TPU v7x, 32 devices: a whole 2x2x4 slice. The times are simulated.
32 devices in a mesh: seq: 4 (over x, core), exp: 8 (over z, y).
Axes of the slice: x: 2, y: 2, z: 4, core: 2. Of those that a mesh axis runs over, the one named last changes fastest.
Arguments:
- xin: bfloat16 [256, 4, 8192], P('seq', None, 'exp'), may hold values from -6 to 6
- zin: bfloat16 [256, 4, 8192], P('seq', None, 'exp'), may hold values from -6 to 6
- conv_weight: float32 [4, 8192], P(None, 'exp'), may hold values from -3 to 3
- conv_bias: float32 [8192], P('exp'), may hold values from -3 to 3
- xproj_weight: bfloat16 [8192, 288], P('exp'), may hold values from -0.0625 to 0.0625
- dtproj_weight: bfloat16 [256, 8192], P(None, 'exp'), may hold values from -0.375 to 0.375
- dt_bias: float32 [8192], P('exp'), may hold values from -5 to -3
- a_log: float32 [16, 8192], P(None, 'exp'), may hold values from -3 to 1
- skip: float32 [8192], P('exp'), may hold values from 0.2 to 1
- out_weight: bfloat16 [8192, 4096], P('exp'), may hold values from -0.0625 to 0.0625
- resid: bfloat16 [256, 4, 4096], P(('seq', 'exp')), may hold values from -6 to 6
- norm_gain: float32 [4096], replicated, may hold values from 0.5 to 1.5
- expert_ids: int32 [256, 4, 2], P(('seq', 'exp')), may hold values from 0 to 7, all different within a row; in each aligned block of 32 rows (0 to 31, 32 to 63, ..., all dimensions but the last counted through in order) at most 16 rows name the same one
- gate_weights: bfloat16 [256, 4, 2], P(('seq', 'exp')), may hold values from 0.19921875 to 1
- w_gate: bfloat16 [8, 4096, 12288], P('exp', None, 'seq'), may hold values from -0.09375 to 0.09375
- w_up: bfloat16 [8, 4096, 12288], P('exp', None, 'seq'), may hold values from -0.09375 to 0.09375
- w_down: bfloat16 [8, 12288, 4096], P('exp', 'seq'), may hold values from -0.0546875 to 0.0546875
Outputs:
- layer_out: bfloat16 [256, 4, 4096], P(('seq', 'exp'))
Inputs may be any that keep to these rules, and one draw needn't show every extreme that they name: `expert_ids`: tokens are ordered by position, then document; in each aligned block of 32 such tokens (the tokens of one device), every expert is named at most 16 times, and in every draw some expert is named exactly 16 times in some block. Each token names 2 different experts.
All inputs are finite; a program needn't handle non-finite values.
Results may differ from a plain program's by a relative error of at most 0.03.
Values may be sent and summed in bfloat16 or wider, within the bound.
A program may use at most 192 MiB of HBM per device.

v0:
```python
import jax
import jax.numpy as jnp
from jax import lax
from jax.sharding import PartitionSpec as P

D = 4096
STATE = 16
CONV = 4
RANK = 256
EXPERTS = 8
TOPK = 2


def passed_along(value, axis, by):
    count = lax.axis_size(axis)
    pairs = [(i, i + by) for i in range(count) if 0 <= i + by < count]
    return lax.ppermute(value, axis, pairs)


def entering(value, axis, join, neutral):
    place = lax.axis_index(axis)
    gathered = jax.tree.map(
        lambda a, kind: lax.all_gather(a.astype(kind), axis), value, (jnp.bfloat16, jnp.bfloat16)
    )
    state = jax.tree.map(lambda a, e: jnp.zeros_like(a) + jnp.asarray(e, a.dtype), value, neutral)

    def one(step, state):
        return join(
            state,
            jax.tree.map(
                lambda a, own: lax.dynamic_index_in_dim(a, step, 0, False).astype(own.dtype),
                gathered,
                value,
            ),
        )

    return lax.fori_loop(0, place, one, state)


def conv_inputs(window, conv_weight, conv_bias, length):
    running = jnp.zeros(window[:length].shape, jnp.float32) + conv_bias
    for offset in range(CONV):
        running = running + conv_weight[offset] * window[offset : offset + length]
    return running


def make_step(decay_rate):

    def advance(carry_state, series_now):
        step_now, input_now, read_now, value_now = series_now
        factor = jnp.exp(step_now[:, None, :] * decay_rate[None])
        carry_state = (
            factor * carry_state + (step_now * value_now)[:, None, :] * input_now[:, :, None]
        )
        return (carry_state, jnp.sum(read_now[:, :, None] * carry_state, axis=1))

    return advance


def chain(earlier, later):
    return (earlier[0] * later[0], later[0] * earlier[1] + later[1])


def slot_select(route_ids, capacity):
    flat_ids = route_ids.reshape(-1)
    onehot = (flat_ids[:, None] == jnp.arange(EXPERTS, dtype=jnp.int32)[None, :]).astype(jnp.int32)
    before = jnp.sum((jnp.cumsum(onehot, axis=0) - onehot) * onehot, axis=1)
    target = flat_ids * capacity + before
    matches = jnp.arange(EXPERTS * capacity, dtype=jnp.int32)[:, None] == target[None, :]
    return matches.reshape(EXPERTS * capacity, route_ids.shape[0], route_ids.shape[1])


def per_device(
    xin,
    zin,
    conv_weight,
    conv_bias,
    xproj_weight,
    dtproj_weight,
    dt_bias,
    a_log,
    skip,
    out_weight,
    resid,
    norm_gain,
    expert_ids,
    gate_weights,
    w_gate,
    w_up,
    w_down,
):
    section = xin.shape[0]
    edge_rows = passed_along(xin[section - (CONV - 1) :], "seq", 1)
    window = jnp.concatenate([edge_rows, xin], axis=0).astype(jnp.float32)
    inner_act = jax.nn.silu(conv_inputs(window, conv_weight, conv_bias, section)).astype(
        jnp.bfloat16
    )
    inner_f = inner_act.astype(jnp.float32)
    projected = jnp.einsum(
        "pbc,cr->pbr", inner_act, xproj_weight, preferred_element_type=jnp.float32
    )
    projected = lax.psum(projected.astype(jnp.bfloat16), "exp").astype(jnp.float32)
    low_rank = projected[..., :RANK].astype(jnp.bfloat16)
    in_state = projected[..., RANK : RANK + STATE]
    out_state = projected[..., RANK + STATE :]
    step_size = jax.nn.softplus(
        jnp.einsum("pbr,rc->pbc", low_rank, dtproj_weight, preferred_element_type=jnp.float32)
        + dt_bias
    )
    decay_rate = -jnp.exp(a_log)
    advance = make_step(decay_rate)
    series = (step_size, in_state, out_state, inner_f)
    zero_state = jnp.zeros((xin.shape[1], STATE, xin.shape[2]), jnp.float32)
    final_local, local_out = lax.scan(advance, zero_state, series)
    total_decay = jnp.exp(jnp.sum(step_size, axis=0)[:, None, :] * decay_rate[None])
    identity = (jnp.ones_like(total_decay), jnp.zeros_like(final_local))
    incoming = entering((total_decay, final_local), "seq", chain, identity)[1]
    ignored, ssm_out = lax.scan(advance, incoming, series)
    mixed_in = ((ssm_out + skip * inner_f) * jax.nn.silu(zin.astype(jnp.float32))).astype(
        jnp.bfloat16
    )
    row_block = mixed_in
    mamba_rows = lax.psum_scatter(
        jnp.einsum("pbc,cd->pbd", row_block, out_weight, preferred_element_type=jnp.float32).astype(
            jnp.bfloat16
        ),
        "exp",
        scatter_dimension=0,
        tiled=True,
    ).astype(jnp.float32)
    hidden_state = resid.astype(jnp.float32) + mamba_rows
    norm_scale = lax.rsqrt(jnp.mean(hidden_state * hidden_state, axis=-1, keepdims=True) + 1e-05)
    normed = (hidden_state * norm_scale * norm_gain).astype(jnp.bfloat16)
    row_count = resid.shape[0] * resid.shape[1]
    capacity = 2 * TOPK * row_count // EXPERTS
    splits = lax.axis_size("exp") // EXPERTS
    tokens = normed.reshape(row_count, D)
    route_ids = expert_ids.reshape(row_count, TOPK)
    gate_vals = gate_weights.reshape(row_count, TOPK)
    matches = slot_select(route_ids, capacity)
    chosen = jnp.sum(matches.astype(jnp.int32), axis=2).astype(jnp.bfloat16)
    outgoing = (
        jnp.dot(chosen, tokens, preferred_element_type=jnp.float32)
        .astype(jnp.bfloat16)
        .reshape(EXPERTS, capacity, D)
    )
    arrived = lax.all_to_all(
        jnp.tile(outgoing, (splits, 1, 1)), "exp", split_axis=0, concat_axis=0, tiled=True
    )
    everything = lax.all_gather(arrived, "seq", axis=0, tiled=True)
    row_block = everything
    expert_row_block = row_block.reshape(-1, D)
    gate_act = jnp.dot(expert_row_block, w_gate[0], preferred_element_type=jnp.float32)
    up_act = jnp.dot(expert_row_block, w_up[0], preferred_element_type=jnp.float32)
    hidden = (jax.nn.silu(gate_act) * up_act).astype(jnp.bfloat16)
    own_rows = lax.psum_scatter(
        jnp.dot(hidden, w_down[0], preferred_element_type=jnp.float32)
        .reshape(lax.axis_size("seq") * arrived.shape[0], capacity, D)
        .astype(jnp.bfloat16),
        "seq",
        scatter_dimension=0,
        tiled=True,
    ).astype(jnp.float32)
    returned = lax.all_to_all(
        own_rows.astype(jnp.bfloat16), "exp", split_axis=0, concat_axis=0, tiled=True
    ).astype(own_rows.dtype)
    summed = jnp.sum(returned.reshape(splits, EXPERTS * capacity, D), axis=0)
    weights = jnp.sum(matches.astype(jnp.float32) * gate_vals.astype(jnp.float32)[None], axis=2)
    expert_out = jnp.dot(weights.T, summed, precision=lax.Precision.HIGHEST)
    return (hidden_state + expert_out.reshape(hidden_state.shape)).astype(jnp.bfloat16)


def solution(mesh):
    placed = (
        P("seq", None, "exp"),
        P("seq", None, "exp"),
        P(None, "exp"),
        P("exp"),
        P("exp", None),
        P(None, "exp"),
        P("exp"),
        P(None, "exp"),
        P("exp"),
        P("exp", None),
        P(("seq", "exp"), None, None),
        P(),
        P(("seq", "exp"), None, None),
        P(("seq", "exp"), None, None),
        P("exp", None, "seq"),
        P("exp", None, "seq"),
        P("exp", "seq", None),
    )
    return jax.shard_map(
        per_device,
        mesh=mesh,
        in_specs=placed,
        out_specs=P(("seq", "exp"), None, None),
        check_vma=False,
    )
```

profile of v0, /device:TPU:0, one launch (start us, length us, event | category | flops | bytes accessed | tf_op | source)
XLA Modules:
  0.0 550.1 jit_solution(11606426716325693040)
XLA Ops:
  6.5 0.8 slice.38
  7.4 2.4 collective-permute-start
  9.7 0.9 fusion.43
  10.7 1.4 maximum_convert_fusion
  12.0 1.7 fusion.39
  13.7 1.1 convolution_convert_fusion.1
  14.9 74.7 %all-reduce.2.cloned.1.call-done = bf16[64,4,288]{2,0,1:T(8,128)(2,1)} async-done(((bf16[64,4,288]{2,0,1:T(8,128)(2,1)}), bf16[64,4,288]{2,0,1:T(8,128)(2,1)}) %all-reduce.2.cloned.1.call-update) | async-done | bytes 147472 | tf_op jit(solution)/shard_map/psum | solution.py:102
  89.6 1.5 fusion.34
  92.4 1.7 fusion.42
  94.2 11.2 %while.37 = (s32[]{:T(128)}, f32[4,16,1024]{2,1,0:T(8,128)S(1)}, f32[64,4,1024]{2,1,0:T(4,128)S(1)}, f32[16,1024]{1,0:T(8,128)S(1)}, f32[64,4,1024]{2,1,0:T(4,12...) while((s32[]{:T(128)}, f32[4,16,1024]{2,1,0:T(8,128)S(1)}, ...), condition=%wide.region_3.4_spmd.clone, body=%wide.region_2.3_spmd.clone.sunk | while | flops 331779 | bytes 705387 | solution.py:114
  105.4 1.0 copy-done.4
  106.4 7.1 %all-gather = bf16[16,16,1024]{2,1,0:T(8,128)(2,1)S(1)} all-gather(bf16[4,16,1024]{2,1,0:T(8,128)(2,1)S(1)} %convert_element_type.103), channel_id=2, replica_groups=mesh['seq'=4,'exp'=8] {'seq'}, dimensions={0}, use_global_device_ids=true | all-gather | bytes 655360 | tf_op jit(solution)/shard_map/all_gather | solution.py:23
  113.6 7.3 %all_gather.13 = bf16[4,4,16,1024]{3,2,1,0:T(8,128)(2,1)S(1)} all-gather(bf16[1,4,16,1024]{3,2,1,0:T(8,128)(2,1)S(1)} %exponential_convert_fusion), channel_id=1, replica_groups=mesh['seq'=4,'exp'=8] {'seq'}, dimensions={0}, use_global_device_ids=true | all-gather | bytes 655360 | tf_op jit(solution)/shard_map/all_gather | solution.py:23
  121.0 141.9 %while.36 = (s32[]{:T(128)}, f32[4,16,1024]{2,1,0:T(8,128)S(1)}, f32[64,4,1024]{2,1,0:T(4,128)}, f32[64,4,1024]{2,1,0:T(4,128)S(1)}, f32[16,1024]{1,0:T(8,128)S(...) while((s32[]{:T(128)}, f32[4,16,1024]{2,1,0:T(8,128)S(1)}, ...), condition=%wide.region_8.9_spmd, body=%wide.region_6.8_spmd.sunk | while | flops 393218 | bytes 755821 | solution.py:118
  121.0 0.7 bitcast_multiply_fusion.4
  141.6 0.7 constant_dynamic-slice_fusion.2
  146.0 0.7 constant_dynamic-slice_fusion.2
  174.6 0.8 constant_dynamic-slice_fusion.2
  176.9 0.8 constant_dynamic-slice_fusion.2
  179.1 0.8 constant_dynamic-slice_fusion.2
  181.3 0.8 constant_dynamic-slice_fusion.2
  183.6 0.8 constant_dynamic-slice_fusion.2
  185.8 0.8 constant_dynamic-slice_fusion.2
  188.1 0.8 constant_dynamic-slice_fusion.2
  190.3 0.8 constant_dynamic-slice_fusion.2
  192.5 0.7 constant_dynamic-slice_fusion.2
  194.8 0.7 constant_dynamic-slice_fusion.2
  197.0 0.7 constant_dynamic-slice_fusion.2
  199.2 0.7 constant_dynamic-slice_fusion.2
  201.4 0.7 constant_dynamic-slice_fusion.2
  203.7 0.7 constant_dynamic-slice_fusion.2
  205.9 0.7 constant_dynamic-slice_fusion.2
  208.1 0.7 constant_dynamic-slice_fusion.2
  228.0 0.7 constant_dynamic-slice_fusion.2
  230.2 0.7 constant_dynamic-slice_fusion.2
  232.4 0.7 constant_dynamic-slice_fusion.2
  234.7 0.7 constant_dynamic-slice_fusion.2
  236.9 0.7 constant_dynamic-slice_fusion.2
  239.1 0.7 constant_dynamic-slice_fusion.2
  241.3 0.7 constant_dynamic-slice_fusion.2
  243.6 0.7 constant_dynamic-slice_fusion.2
  245.8 0.7 constant_dynamic-slice_fusion.2
  248.0 0.7 constant_dynamic-slice_fusion.2
  250.2 0.7 constant_dynamic-slice_fusion.2
  252.5 0.7 constant_dynamic-slice_fusion.2
  254.7 0.7 constant_dynamic-slice_fusion.2
  256.9 0.7 constant_dynamic-slice_fusion.2
  259.1 0.7 constant_dynamic-slice_fusion.2
  261.4 0.7 constant_dynamic-slice_fusion.2
  262.9 2.1 fusion.29
  265.0 5.7 %fusion.15 = bf16[4,8,8,4096]{3,2,1,0:T(8,128)(2,1)S(1)} fusion(bf16[1024,4096]{1,0:T(8,128)(2,1)} %param.32, bf16[64,4,1024]{2,1,0:T(4,128)(2,1)S(1)} %fusion.29), kind=kOutput, calls=%fused_computation.25 | convolution fusion | flops 2148532224 | bytes 11010048 | tf_op jit(solution)/shard_map/pbc,cd->pbd/dot_general | solution.py:124
  270.8 1.6 copy.92
  273.5 65.4 %reduce-scatter.7.cloned.1.call-done = bf16[8,16384]{1,0:T(8,128)(2,1)} async-done(((bf16[64,16384]{1,0:T(8,128)(2,1)}), bf16[8,16384]{1,0:T(8,128)(2,1)}) %reduce-scatter.7.cloned.1.call-update) | async-done | bytes 262160
  338.9 1.3 multiply_reduce_fusion.1
  340.3 1.1 multiply_convert_fusion.1
  342.1 28.1 %all_to_all.10 = bf16[8,16,4096]{2,1,0:T(8,128)(2,1)} all-to-all(bf16[8,16,4096]{2,1,0:T(8,128)(2,1)S(1)} %bitcast.110), channel_id=1, replica_groups=mesh['seq'=4,'exp'=8] {'exp'}, dimensions={0} | all-to-all | bytes 2097152 | tf_op jit(solution)/shard_map/all_to_all | solution.py:147
  370.3 33.6 %all-gather.3.cloned.1.call-done = bf16[32,16,4096]{2,1,0:T(8,128)(2,1)} async-done(((bf16[8,16,4096]{2,1,0:T(8,128)(2,1)}), bf16[32,16,4096]{2,1,0:T(8,128)(2,1)}) %all-gather.3.cloned.1.call-update) | async-done | bytes 4194320 | tf_op jit(solution)/shard_map/all_gather | solution.py:150
  403.9 21.6 %fusion.5 = f32[512,3072]{1,0:T(8,128)} fusion(bf16[512,4096]{1,0:T(8,128)(2,1)} %bitcast.121, bf16[1,4096,3072]{2,1,0:T(8,128)(2,1)} %param.37), kind=kOutput, calls=%fused_computation.18 | convolution fusion | flops 12884901888 | bytes 35651584 | tf_op jit(solution)/shard_map/dot_general | solution.py:153
  425.5 20.3 %multiply_convert_fusion = bf16[512,3072]{1,0:T(8,128)(2,1)} fusion(f32[512,3072]{1,0:T(8,128)} %fusion.5, bf16[512,4096]{1,0:T(8,128)(2,1)S(1)} %bitcast.122, bf16[1,4096,3072]{2,1,0:T(8,128)(2,1)} %param.38), kind=kOutput, calls=%fused_computation.22 | convolution fusion | flops 12894339072 | bytes 38797312 | tf_op jit(solution)/shard_map/dot_general | solution.py:154
  445.9 20.2 %fusion.9 = bf16[32,16,4096]{2,1,0:T(8,128)(2,1)} fusion(bf16[32,16,3072]{2,1,0:T(8,128)(2,1)} %bitcast.123, bf16[1,3072,4096]{2,1,0:T(8,128)(2,1)} %param.39), kind=kOutput, calls=%fused_computation.23 | convolution fusion | flops 12886999040 | bytes 32505856 | tf_op jit(solution)/shard_map/dot_general | solution.py:157
  466.1 44.7 %reduce-scatter.5.cloned.1.call-done = bf16[8,16,4096]{2,1,0:T(8,128)(2,1)} async-done(((bf16[32,16,4096]{2,1,0:T(8,128)(2,1)}), bf16[8,16,4096]{2,1,0:T(8,128)(2,1)}) %reduce-scatter.5.cloned.1.call-update) | async-done | bytes 1048592 | tf_op jit(solution)/shard_map/reduce_scatter | solution.py:156
  510.8 5.5 %all-to-all-start.1 = ((bf16[8,16,4096]{2,1,0:T(8,128)(2,1)}), bf16[8,16,4096]{2,1,0:T(8,128)(2,1)S(1)}, u32[]{:S(2)}, u32[]{:S(2)}) async-start(bf16[8,16,4096]{2,1,0:T(8,128)(2,1)} %reduce-scatter.5.cloned.1.call-done), calls=%async_computation.2 | async-start | bytes 2097152 | tf_op jit(solution)/shard_map/all_to_all | solution.py:164
  516.6 25.5 %all-to-all-done.1 = bf16[8,16,4096]{2,1,0:T(8,128)(2,1)S(1)} async-done(((bf16[8,16,4096]{2,1,0:T(8,128)(2,1)}), bf16[8,16,4096]{2,1,0:T(8,128)(2,1)S(1)}, u32[]{:S(2)}, u32[]{:S(2)}) %all-to-all-start.1) | async-done | bytes 1048608 | tf_op jit(solution)/shard_map/all_to_all | solution.py:164
  542.7 0.9 copy.85
  (667 shorter events, 128.1 us)
Async XLA Ops:
  6.5 7.2 %copy-start = (bf16[1024,288]{0,1:T(8,128)(2,1)S(1)}, bf16[1024,288]{0,1:T(8,128)(2,1)}, u32[]{:S(2)}) copy-start(bf16[1024,288]{0,1:T(8,128)(2,1)} %param.27) | copy-start | bytes 1769476
  6.5 8.4 %copy-start.5 = (f32[16,1024]{1,0:T(8,128)S(1)}, f32[16,1024]{1,0:T(8,128)}, u32[]{:S(2)}) copy-start(f32[16,1024]{1,0:T(8,128)} %param.30) | copy-start | bytes 196612
  6.5 83.1 %copy-start.8 = (f32[1024]{0:T(1024)S(1)}, f32[1024]{0:T(1024)}, u32[]{:S(2)}) copy-start(f32[1024]{0:T(1024)} %param.29) | copy-start | bytes 12292
  6.5 83.1 %all-reduce.2.cloned.1.call-start = ((), (), s32[]{:S(2)}) async-start(), calls=%async_computation.4 | async-start | bytes 393216 | tf_op jit(solution)/shard_map/psum | solution.py:102
  7.4 3.3 collective-permute-start
  14.9 324.1 %reduce-scatter.7.cloned.1.call-start = ((), (), s32[]{:S(2)}) async-start(), calls=%async_computation.7 | async-start | bytes 2359296
  94.2 168.7 %copy-start.9 = (f32[1024]{0:T(1024)S(1)}, f32[1024]{0:T(1024)}, u32[]{:S(2)}) copy-start(f32[1024]{0:T(1024)} %param.31) | copy-start | bytes 12292
  105.4 1.0 copy-start.4
  270.8 1.7 copy-start.7
  270.8 68.1 %copy-start.2 = (bf16[8,4,4096]{2,1,0:T(4,128)(2,1)S(1)}, bf16[8,4,4096]{2,1,0:T(4,128)(2,1)}, u32[]{:S(2)}) copy-start(bf16[8,4,4096]{2,1,0:T(4,128)(2,1)} %param.33) | copy-start | bytes 786436
  270.8 69.5 %copy-start.6 = (f32[4096]{0:T(1024)S(1)}, f32[4096]{0:T(1024)}, u32[]{:S(2)}) copy-start(f32[4096]{0:T(1024)} %param.34) | copy-start | bytes 49156
  272.4 131.5 %all-gather.3.cloned.1.call-start = ((), (), s32[]{:S(2)}) async-start(), calls=%async_computation.5 | async-start | bytes 5242880 | tf_op jit(solution)/shard_map/all_gather | solution.py:150
  370.3 140.5 %reduce-scatter.5.cloned.1.call-start = ((), (), s32[]{:S(2)}) async-start(), calls=%async_computation.6 | async-start | bytes 5242880 | tf_op jit(solution)/shard_map/reduce_scatter | solution.py:156
  403.9 21.6 %copy-start.11 = (bf16[32,16,4096]{2,1,0:T(8,128)(2,1)S(1)}, bf16[32,16,4096]{2,1,0:T(8,128)(2,1)}, u32[]{:S(2)}) copy-start(bf16[32,16,4096]{2,1,0:T(8,128)(2,1)} %all-gather.3.cloned.1.call-done) | copy-start | bytes 12582916
  445.8 97.7 %copy-start.1 = (bf16[1024,288]{0,1:T(8,128)(2,1)S(1)}, bf16[1024,288]{0,1:T(8,128)(2,1)}, u32[]{:S(2)}) copy-start(bf16[1024,288]{0,1:T(8,128)(2,1)} %param.27) | copy-start | bytes 1769476
  466.1 50.2 %copy-start.10 = (bf16[8,4,2]{0,2,1:T(2,128)(2,1)S(1)}, bf16[8,4,2]{0,2,1:T(2,128)(2,1)}, u32[]{:S(2)}) copy-start(bf16[8,4,2]{0,2,1:T(2,128)(2,1)} %param.36) | copy-start | bytes 388
  466.1 76.0 %copy-start.3 = (bf16[8,16384]{1,0:T(8,128)(2,1)S(1)}, bf16[8,16384]{1,0:T(8,128)(2,1)}, u32[]{:S(2)}) copy-start(bf16[8,16384]{1,0:T(8,128)(2,1)} %reduce-scatter.7.cloned.1.call-done) | copy-start | bytes 786436
  510.8 31.3 %all-to-all-start.1 = ((bf16[8,16,4096]{2,1,0:T(8,128)(2,1)}), bf16[8,16,4096]{2,1,0:T(8,128)(2,1)S(1)}, u32[]{:S(2)}, u32[]{:S(2)}) async-start(bf16[8,16,4096]{2,1,0:T(8,128)(2,1)} %reduce-scatter.5.cloned.1.call-done), calls=%async_computation.2 | async-start | bytes 2097152 | tf_op jit(solution)/shard_map/all_to_all | solution.py:164
Sparse Core Ops, SparseCore 0:
  15.0 74.5 all-reduce.1
  272.5 66.3 reduce-scatter.6
  370.4 33.4 all-gather.2
  466.2 44.5 reduce-scatter.4
where the time goes:
time: 558 us; the launch traced here: 550 us
  waiting for transfers between devices  244 us (44%)
  local copies, waits for them, and re-layouts  96.2 us (17%)
  matrix products  71.6 us (13%)
  other arithmetic  71.3 us (13%)
  blocking collectives  42.5 us (8%)
  between operations  13.4 us (2%)
  starting transfers between devices  8 us (1%)
    psum x1, waiting for transfers between devices, per_device(): lax.psum(projected.astype(jnp.bfloat16), 'exp').astype(jnp.float32)  74.7 us
    unnamed x5, waiting for transfers between devices  65.5 us
    dynamic_slice x64, local copies, waits for them, and re-layouts, per_device(): final_local, local_out = lax.scan(advance, zero_state, series)  47.2 us
    mul x128, other arithmetic, advance(): step_now * value_now  47 us
    reduce_scatter x1, waiting for transfers between devices, per_device(): lax.psum_scatter(jnp.dot(hidden, w_down[0], preferred_element_type=jnp.fl...  44.7 us
    dynamic_update_slice x64, local copies, waits for them, and re-layouts, per_device(): ignored, ssm_out = lax.scan(advance, incoming, series)  38.7 us
    all_gather x1, waiting for transfers between devices, per_device(): everything = lax.all_gather(arrived, 'seq', axis=0, tiled=True)  33.6 us
    all_to_all x1, blocking collectives, per_device(): lax.all_to_all(jnp.tile(outgoing, (splits, 1, 1)), 'exp', split_axis=0, c...  28.1 us
  transfers between devices with their start and end apart: 6, of which 5 were waited for; matrix products, arithmetic and copies ran while one was open for 0% of the time, Pallas kernels for 0%

commit v1 on v0

v1 whole, which is shorter than its diff:
```python
import functools

import jax
import jax.numpy as jnp
from jax import lax
from jax.experimental import pallas as pl
from jax.experimental.pallas import tpu as pltpu
from jax.sharding import PartitionSpec as P

D = 4096
STATE = 16
CONV = 4
RANK = 256
EXPERTS = 8
TOPK = 2


def passed_along(value, axis, by):
    count = lax.axis_size(axis)
    pairs = [(i, i + by) for i in range(count) if 0 <= i + by < count]
    return lax.ppermute(value, axis, pairs)


def conv_inputs(window, conv_weight, conv_bias, length):
    running = jnp.zeros(window[:length].shape, jnp.float32) + conv_bias
    for offset in range(CONV):
        running = running + conv_weight[offset] * window[offset : offset + length]
    return running


MESH = pl.DeviceIdType.MESH
VMEM = pl.BlockSpec(memory_space=pltpu.VMEM)


def remote(src, dst, send, recv, where):
    return pltpu.make_async_remote_copy(
        src_ref=src,
        dst_ref=dst,
        send_sem=send,
        recv_sem=recv,
        device_id=where,
        device_id_type=MESH,
    )


def greet(others):
    barrier = pltpu.get_barrier_semaphore()
    for other in others:
        pl.semaphore_signal(barrier, inc=1, device_id=other, device_id_type=MESH)
    pl.semaphore_wait(barrier, len(others))


def total_of(first, rest):
    total = first.astype(jnp.float32)
    for value in rest:
        total = total + value.astype(jnp.float32)
    return total


def communicating(kernel, number, out, scratch, operand):
    return pl.pallas_call(
        kernel,
        out_shape=out,
        in_specs=[VMEM],
        out_specs=VMEM,
        scratch_shapes=scratch,
        compiler_params=pltpu.CompilerParams(
            collective_id=number, has_side_effects=True, vmem_limit_bytes=40 * 2**20
        ),
    )(operand)


def dma(count):
    return pltpu.SemaphoreType.DMA((count,))


def sum_kernel(n, x, out, arrived, spread, send1, recv1, send2, recv2):
    row, me = lax.axis_index("seq"), lax.axis_index("exp")
    greet([(row, lax.rem(me + k, n)) for k in range(1, n)])
    copies = []
    for k in range(1, n):
        peer = lax.rem(me + k, n)
        copies.append(
            remote(x.at[peer], arrived.at[k - 1], send1.at[k - 1], recv1.at[k - 1], (row, peer))
        )
        copies[-1].start()
    for copy in copies:
        copy.wait_recv()
    spread[me] = total_of(x[me], [arrived[k] for k in range(n - 1)]).astype(jnp.bfloat16)
    again = []
    for k in range(1, n):
        peer = lax.rem(me + k, n)
        again.append(
            remote(spread.at[me], spread.at[me], send2.at[k - 1], recv2.at[k - 1], (row, peer))
        )
        again[-1].start()
    for copy in again:
        copy.wait_recv()
    out[...] = spread[...]
    for copy in copies + again:
        copy.wait_send()


def summed_over_exp(value):
    n = lax.axis_size("exp")
    rows, columns = value.shape
    blocks = value.reshape(n, rows // n, columns)
    return communicating(
        functools.partial(sum_kernel, n),
        0,
        jax.ShapeDtypeStruct(blocks.shape, jnp.bfloat16),
        [
            pltpu.VMEM((n - 1,) + blocks.shape[1:], jnp.bfloat16),
            pltpu.VMEM(blocks.shape, jnp.bfloat16),
        ]
        + [dma(n - 1)] * 4,
        blocks,
    ).reshape(rows, columns)


def scatter_kernel(outer, inner, parts, x, out, first, middle, second, send1, recv1, send2, recv2):
    row, me = lax.axis_index("seq"), lax.axis_index("exp")
    o, i = me // inner, lax.rem(me, inner)
    near = [lax.rem(i + d, inner) for d in range(1, inner)]
    far = [lax.rem(o + d, outer) for d in range(1, outer)]
    greet([(row, o * inner + p) for p in near] + [(row, p * inner + i) for p in far])
    width = x.shape[3] // parts
    ones, twos = [], []
    for c in range(parts):
        columns = pl.ds(c * width, width)
        ones.append([])
        for d, p in enumerate(near):
            at = c * len(near) + d
            ones[c].append(
                remote(
                    x.at[:, p, :, columns],
                    first.at[d, :, :, columns],
                    send1.at[at],
                    recv1.at[at],
                    (row, o * inner + p),
                )
            )
            ones[c][d].start()
    for c in range(parts):
        columns = pl.ds(c * width, width)
        for copy in ones[c]:
            copy.wait_recv()
        for q in range(outer):
            middle[q, :, columns] = total_of(
                x[q, i, :, columns], [first[d, q, :, columns] for d in range(len(near))]
            ).astype(jnp.bfloat16)
        twos.append([])
        for d, p in enumerate(far):
            at = c * len(far) + d
            twos[c].append(
                remote(
                    middle.at[p, :, columns],
                    second.at[d, :, columns],
                    send2.at[at],
                    recv2.at[at],
                    (row, p * inner + i),
                )
            )
            twos[c][d].start()
    for c in range(parts):
        columns = pl.ds(c * width, width)
        for copy in twos[c]:
            copy.wait_recv()
        out[:, columns] = total_of(
            middle[o, :, columns], [second[d, :, columns] for d in range(len(far))]
        )
    for copy in sum(ones, []) + sum(twos, []):
        copy.wait_send()


def scattered_over_exp(value):
    n = lax.axis_size("exp")
    outer, parts = 4, 4
    inner = n // outer
    rows, columns = value.shape
    rows = rows // n
    near, far = parts * (inner - 1), parts * (outer - 1)
    return communicating(
        functools.partial(scatter_kernel, outer, inner, parts),
        1,
        jax.ShapeDtypeStruct((rows, columns), jnp.float32),
        [
            pltpu.VMEM((inner - 1, outer, rows, columns), jnp.bfloat16),
            pltpu.VMEM((outer, rows, columns), jnp.bfloat16),
            pltpu.VMEM((outer - 1, rows, columns), jnp.bfloat16),
            dma(near),
            dma(near),
            dma(far),
            dma(far),
        ],
        value.reshape(outer, inner, rows, columns),
    )


def places(n_seq, n_exp):
    row, me = lax.axis_index("seq"), lax.axis_index("exp")
    count = n_seq // 2
    chip, core = row // 2, lax.rem(row, 2)
    chips = [lax.rem(chip + d, count) for d in range(count)]
    back = [lax.rem(chip + count - d, count) for d in range(count)]
    partner = (chip * 2 + 1 - core, me)
    greet(
        [(row, lax.rem(me + k, n_exp)) for k in range(1, n_exp)]
        + [(p * 2 + core, me) for p in chips[1:]]
        + [partner]
    )
    return row, me, count, core, chips, back, partner


def dispatch_kernel(n_seq, n_exp, x, out, send1, recv1, send2, recv2, send3, recv3):
    row, me, count, core, chips, back, partner = places(n_seq, n_exp)
    out[row, me] = x[me]
    ones, twos, threes = [], [], []
    for k in range(1, n_exp):
        peer = lax.rem(me + k, n_exp)
        ones.append(
            remote(x.at[peer], out.at[row, me], send1.at[k - 1], recv1.at[k - 1], (row, peer))
        )
        ones[-1].start()

    def shared(origin, source, at):
        block = out.at[origin, source]
        threes.append(remote(block, block, send3.at[at], recv3.at[at], partner))
        threes[-1].start()

    for k in range(n_exp):
        if k > 0:
            ones[k - 1].wait_recv()
        source = lax.rem(me + n_exp - k, n_exp)
        block = out.at[row, source]
        for d in range(1, count):
            at = (d - 1) * n_exp + k
            twos.append(
                remote(block, block, send2.at[at], recv2.at[at], (chips[d] * 2 + core, me))
            )
            twos[-1].start()
        shared(row, source, k)
    for k in range(n_exp):
        source = lax.rem(me + n_exp - k, n_exp)
        for d in range(1, count):
            twos[k * (count - 1) + d - 1].wait_recv()
            shared(back[d] * 2 + core, source, d * n_exp + k)
    for copy in threes:
        copy.wait_recv()
    for copy in ones + twos + threes:
        copy.wait_send()


def dispatched(value):
    n_seq, n_exp = lax.axis_size("seq"), lax.axis_size("exp")
    count = n_seq // 2
    across = (count - 1) * n_exp
    return communicating(
        functools.partial(dispatch_kernel, n_seq, n_exp),
        2,
        jax.ShapeDtypeStruct((n_seq,) + value.shape, jnp.bfloat16),
        [dma(n_exp - 1)] * 2 + [dma(across)] * 2 + [dma(count * n_exp)] * 2,
        value,
    )


def return_kernel(
    n_seq, n_exp, x, out, near, pair, far, total, send1, recv1, send2, recv2, send3, recv3
):
    row, me, count, core, chips, back, partner = places(n_seq, n_exp)
    order = list(range(1, n_exp)) + [0]
    targets = [lax.rem(me + k, n_exp) for k in order]
    ones, twos, threes = [], [], []
    for s in range(n_exp):
        ones.append([])
        for d in range(count):
            at = s * count + d
            ones[s].append(
                remote(
                    x.at[chips[d] * 2 + 1 - core, targets[s]],
                    near.at[chips[d], targets[s]],
                    send1.at[at],
                    recv1.at[at],
                    partner,
                )
            )
            ones[s][d].start()
    for s in range(n_exp + 1):
        if s < n_exp:
            twos.append([])
            for d in list(range(1, count)) + [0]:
                ones[s][d].wait_recv()
                place = (chips[d], targets[s])
                pair[place] = total_of(
                    x[chips[d] * 2 + core, targets[s]], [near[place]]
                ).astype(jnp.bfloat16)
                if d > 0:
                    at = s * (count - 1) + d - 1
                    twos[s].append(
                        remote(
                            pair.at[place],
                            far.at[d - 1, targets[s]],
                            send2.at[at],
                            recv2.at[at],
                            (chips[d] * 2 + core, me),
                        )
                    )
                    twos[s][-1].start()
        if s > 0:
            t = s - 1
            for copy in twos[t]:
                copy.wait_recv()
            block = total_of(
                pair[chips[0], targets[t]], [far[d, targets[t]] for d in range(count - 1)]
            ).astype(jnp.bfloat16)
            if order[t] == 0:
                out[me] = block
            else:
                total[targets[t]] = block
                threes.append(
                    remote(
                        total.at[targets[t]],
                        out.at[me],
                        send3.at[t],
                        recv3.at[t],
                        (row, targets[t]),
                    )
                )
                threes[-1].start()
    for copy in threes:
        copy.wait_recv()
    for copy in sum(ones, []) + sum(twos, []) + threes:
        copy.wait_send()


def sent_back(value):
    n_seq, n_exp = lax.axis_size("seq"), lax.axis_size("exp")
    count = n_seq // 2
    block = value.shape[1:]
    return communicating(
        functools.partial(return_kernel, n_seq, n_exp),
        3,
        jax.ShapeDtypeStruct(block, jnp.bfloat16),
        [
            pltpu.VMEM((count,) + block, jnp.bfloat16),
            pltpu.VMEM((count,) + block, jnp.bfloat16),
            pltpu.VMEM((count - 1,) + block, jnp.bfloat16),
            pltpu.VMEM(block, jnp.bfloat16),
        ]
        + [dma(count * n_exp)] * 2
        + [dma((count - 1) * n_exp)] * 2
        + [dma(n_exp - 1)] * 2,
        value,
    )


def scan_kernel(step, given, feed, decay, *rest):
    start, read, result = rest if len(rest) == 3 else (None, None, rest[0])
    wide = step.shape[2]
    rates = decay[...]

    def across(tile):
        return jnp.concatenate([tile] * (wide // 128), axis=1)

    def eight(block, state):
        rows = pl.ds(pl.multiple_of(block * 8, 8), 8)
        steps, values = step[0, rows, :], given[0, rows, :]
        outs = []
        for r in range(8):
            state = jnp.exp(steps[r : r + 1] * rates) * state + values[r : r + 1] * across(
                feed[0, block * 8 + r]
            )
            if read is not None:
                outs.append(
                    jnp.sum(across(read[0, block * 8 + r]) * state, axis=0, keepdims=True)
                )
        if read is not None:
            result[0, rows, :] = jnp.concatenate(outs, axis=0)
        return state

    first = jnp.zeros(rates.shape, jnp.float32) if start is None else start[0]
    last = lax.fori_loop(0, step.shape[1] // 8, eight, first)
    if read is None:
        result[0] = last


def run_scan(step, given, feed, decay, start=None, read=None):
    docs, length, channels = step.shape
    wide = 512
    series = pl.BlockSpec((1, length, wide), lambda b, c: (b, 0, c))
    states = pl.BlockSpec((1, length, STATE, 128), lambda b, c: (b, 0, 0, 0))
    rates = pl.BlockSpec((STATE, wide), lambda b, c: (0, c))
    whole = pl.BlockSpec((1, STATE, wide), lambda b, c: (b, 0, c))
    operands, specs = [step, given, feed, decay], [series, series, states, rates]
    if read is None:
        shape, out = (docs, STATE, channels), whole
    else:
        operands, specs = operands + [start, read], specs + [whole, states]
        shape, out = step.shape, series
    return pl.pallas_call(
        scan_kernel,
        grid=(docs, channels // wide),
        out_shape=jax.ShapeDtypeStruct(shape, jnp.float32),
        in_specs=specs,
        out_specs=out,
        compiler_params=pltpu.CompilerParams(vmem_limit_bytes=32 * 2**20),
    )(*operands)


def slot_select(route_ids, capacity):
    flat_ids = route_ids.reshape(-1)
    onehot = (flat_ids[:, None] == jnp.arange(EXPERTS, dtype=jnp.int32)[None, :]).astype(jnp.int32)
    before = jnp.sum((jnp.cumsum(onehot, axis=0) - onehot) * onehot, axis=1)
    target = flat_ids * capacity + before
    matches = jnp.arange(EXPERTS * capacity, dtype=jnp.int32)[:, None] == target[None, :]
    return matches.reshape(EXPERTS * capacity, route_ids.shape[0], route_ids.shape[1])


def per_device(
    xin,
    zin,
    conv_weight,
    conv_bias,
    xproj_weight,
    dtproj_weight,
    dt_bias,
    a_log,
    skip,
    out_weight,
    resid,
    norm_gain,
    expert_ids,
    gate_weights,
    w_gate,
    w_up,
    w_down,
):
    section = xin.shape[0]
    edge_rows = passed_along(xin[section - (CONV - 1) :], "seq", 1)
    window = jnp.concatenate([edge_rows, xin], axis=0).astype(jnp.float32)
    inner_act = jax.nn.silu(conv_inputs(window, conv_weight, conv_bias, section)).astype(
        jnp.bfloat16
    )
    inner_f = inner_act.astype(jnp.float32)
    docs, channels = xin.shape[1], xin.shape[2]
    count = section * docs
    padded = jnp.pad(xproj_weight, ((0, 0), (0, -xproj_weight.shape[1] % 128)))
    projected = jnp.dot(
        inner_act.reshape(count, channels), padded, preferred_element_type=jnp.float32
    )
    projected = summed_over_exp(projected.astype(jnp.bfloat16))
    projected = projected.reshape(section, docs, -1).transpose(1, 0, 2)
    low_rank = projected[..., :RANK]
    states = projected[..., RANK : RANK + 2 * STATE].astype(jnp.float32)
    spread = jnp.broadcast_to(states[..., None], states.shape + (128,))
    in_state, out_state = spread[:, :, :STATE], spread[:, :, STATE:]
    inner_t = inner_f.transpose(1, 0, 2)
    step_size = jax.nn.softplus(
        jnp.einsum("bpr,rc->bpc", low_rank, dtproj_weight, preferred_element_type=jnp.float32)
        + dt_bias
    )
    decay_rate = -jnp.exp(a_log)
    given = step_size * inner_t
    final_local = run_scan(step_size, given, in_state, decay_rate)
    all_steps = lax.all_gather(jnp.sum(step_size, axis=1), "seq")
    all_finals = lax.all_gather(final_local.astype(jnp.bfloat16), "seq")
    place = lax.axis_index("seq")
    incoming = jnp.zeros_like(final_local)
    for q in range(lax.axis_size("seq") - 1):
        through = jnp.exp(all_steps[q][:, None, :] * decay_rate[None])
        incoming = jnp.where(
            q < place, through * incoming + all_finals[q].astype(jnp.float32), incoming
        )
    ssm_out = run_scan(step_size, given, in_state, decay_rate, incoming, out_state)
    mixed_in = (
        (ssm_out.transpose(1, 0, 2) + skip * inner_f) * jax.nn.silu(zin.astype(jnp.float32))
    ).astype(jnp.bfloat16)
    mamba_rows = scattered_over_exp(
        jnp.dot(
            mixed_in.reshape(count, channels), out_weight, preferred_element_type=jnp.float32
        ).astype(jnp.bfloat16)
    ).reshape(resid.shape)
    hidden_state = resid.astype(jnp.float32) + mamba_rows
    norm_scale = lax.rsqrt(jnp.mean(hidden_state * hidden_state, axis=-1, keepdims=True) + 1e-05)
    normed = (hidden_state * norm_scale * norm_gain).astype(jnp.bfloat16)
    row_count = resid.shape[0] * resid.shape[1]
    capacity = 2 * TOPK * row_count // EXPERTS
    splits = lax.axis_size("exp") // EXPERTS
    tokens = normed.reshape(row_count, D)
    route_ids = expert_ids.reshape(row_count, TOPK)
    gate_vals = gate_weights.reshape(row_count, TOPK)
    matches = slot_select(route_ids, capacity)
    chosen = jnp.sum(matches.astype(jnp.int32), axis=2).astype(jnp.bfloat16)
    outgoing = (
        jnp.dot(chosen, tokens, preferred_element_type=jnp.float32)
        .astype(jnp.bfloat16)
        .reshape(EXPERTS, capacity, D)
    )
    row_block = dispatched(jnp.tile(outgoing, (splits, 1, 1)))
    expert_row_block = row_block.reshape(-1, D)
    gate_act = jnp.dot(expert_row_block, w_gate[0], preferred_element_type=jnp.float32)
    up_act = jnp.dot(expert_row_block, w_up[0], preferred_element_type=jnp.float32)
    hidden = (jax.nn.silu(gate_act) * up_act).astype(jnp.bfloat16)
    returned = sent_back(
        jnp.dot(hidden, w_down[0], preferred_element_type=jnp.float32)
        .astype(jnp.bfloat16)
        .reshape(row_block.shape)
    ).astype(jnp.float32)
    summed = jnp.sum(returned.reshape(splits, EXPERTS * capacity, D), axis=0)
    weights = jnp.sum(matches.astype(jnp.float32) * gate_vals.astype(jnp.float32)[None], axis=2)
    expert_out = jnp.dot(weights.T, summed, precision=lax.Precision.HIGHEST)
    return (hidden_state + expert_out.reshape(hidden_state.shape)).astype(jnp.bfloat16)


def solution(mesh):
    placed = (
        P("seq", None, "exp"),
        P("seq", None, "exp"),
        P(None, "exp"),
        P("exp"),
        P("exp", None),
        P(None, "exp"),
        P("exp"),
        P(None, "exp"),
        P("exp"),
        P("exp", None),
        P(("seq", "exp"), None, None),
        P(),
        P(("seq", "exp"), None, None),
        P(("seq", "exp"), None, None),
        P("exp", None, "seq"),
        P("exp", None, "seq"),
        P("exp", "seq", None),
    )
    return jax.shard_map(
        per_device,
        mesh=mesh,
        in_specs=placed,
        out_specs=P(("seq", "exp"), None, None),
        check_vma=False,
    )
```

time: 558 us -> 233 us (0.42); the launches traced: 550 us -> 231 us
  waiting for transfers between devices: 244 us -> 0.01 us
  Pallas kernels: 0 us -> 134 us
  local copies, waits for them, and re-layouts: 96.2 us -> 8.11 us
  other arithmetic: 71.3 us -> 6.55 us
  blocking collectives: 42.5 us -> 12.5 us
  between operations: 13.4 us -> 0.5 us
  starting transfers between devices: 8 us -> 2.36 us
    pallas_call x0 -> x6, Pallas kernels: none -> 134 us  [the longest x4 122 us: communicating(): pl.pallas_call(kernel, out_shape=out, in_specs=[VMEM], out_specs=VMEM, sc...]
    psum x1 -> x0, waiting for transfers between devices: 74.7 us -> none  [per_device(): lax.psum(projected.astype(jnp.bfloat16), 'exp').astype(jnp.float32)]
    unnamed x5 -> x0, waiting for transfers between devices: 65.5 us -> none
    dynamic_slice x64 -> x0, local copies, waits for them, and re-layouts: 47.2 us -> none  [per_device(): final_local, local_out = lax.scan(advance, zero_state, series)]
    mul x128 -> x0, other arithmetic: 47 us -> none  [advance(): step_now * value_now]
    reduce_scatter x1 -> x0, waiting for transfers between devices: 44.7 us -> none  [per_device(): lax.psum_scatter(jnp.dot(hidden, w_down[0], preferred_element_type=jnp.fl...]
    dynamic_update_slice x64 -> x0, local copies, waits for them, and re-layouts: 38.7 us -> none  [per_device(): ignored, ssm_out = lax.scan(advance, incoming, series)]
    all_gather x1 -> x0, waiting for transfers between devices: 33.6 us -> none  [per_device(): everything = lax.all_gather(arrived, 'seq', axis=0, tiled=True)]
  transfers between devices with their start and end apart: 6 -> 1, of which waited for: 5 -> 0; matrix products, arithmetic and copies ran while one was open for 0% -> 2% of each run, Pallas kernels for 0% -> 0%
where the time goes in v1:
time: 233 us; the launch traced here: 231 us
  Pallas kernels  134 us (58%)
  matrix products  67.2 us (29%)
  blocking collectives  12.5 us (5%)
  local copies, waits for them, and re-layouts  8.11 us (3%)
  other arithmetic  6.55 us (3%)
  starting transfers between devices  2.36 us (1%)
    pallas_call x4, Pallas kernels, communicating(): pl.pallas_call(kernel, out_shape=out, in_specs=[VMEM], out_specs=VMEM, sc...  122 us
    dot_general x1, matrix products, per_device(): jnp.dot(expert_row_block, w_up[0], preferred_element_type=jnp.float32)  20.3 us
    dot_general x1, matrix products, per_device(): jnp.dot(hidden, w_down[0], preferred_element_type=jnp.float32)  18.9 us
    dot_general x1, matrix products, per_device(): jnp.dot(expert_row_block, w_gate[0], preferred_element_type=jnp.float32)  18.5 us
    pallas_call x2, Pallas kernels, run_scan(): pl.pallas_call(scan_kernel, grid=(docs, channels // wide), out_shape=jax....  11.9 us
    all_gather x1, blocking collectives, per_device(): all_finals = lax.all_gather(final_local.astype(jnp.bfloat16), 'seq')  7.1 us
    dot_general x1, matrix products, per_device(): jnp.dot(mixed_in.reshape(count, channels), out_weight, preferred_element_...  5.76 us
    all_gather x1, blocking collectives, per_device(): all_steps = lax.all_gather(jnp.sum(step_size, axis=1), 'seq')  5.41 us
  transfers between devices with their start and end apart: 1, of which 0 were waited for; matrix products, arithmetic and copies ran while one was open for 2% of the time, Pallas kernels for 0%

profile of v1, /device:TPU:0, one launch (start us, length us, event | category | flops | bytes accessed | tf_op | source)
XLA Modules:
  0.0 231.1 jit_solution(16949734523271569264)
XLA Ops:
  0.0 0.0 copy-start
  0.0 1.3 copy.66
  1.3 0.0 copy-start.16
  1.3 2.4 %collective-permute-start = (bf16[3,4,1024]{2,0,1:T(4,128)(2,1)S(1)}, bf16[3,4,1024]{2,0,1:T(4,128)(2,1)S(1)}, u32[]{:S(2)}, u32[]{:S(2)}) collective-permute-start(bf16[3,4,1024]{2,0,1:T(4,128)(2,1)S(1)} %slice.87), channel_id=1, source_target_pairs={{0,8},{8,16},{16,24},{1,9},{9,17},{17,25},{2,10},{10,18},{18,26},{... | collective-permute-start | bytes 73736 | tf_op jit(solution)/shard_map/ppermute | solution.py:21
  3.7 0.8 copy.74
  4.5 0.7 broadcast_multiply_fusion
  5.1 0.9 fusion.38
  6.0 0.0 copy-start.5
  6.0 0.0 copy-start.7
  6.1 0.9 exponential_negate_fusion.decay
  6.9 0.1 eq.30
  7.0 0.1 fusion.31
  7.1 0.1 reduce_window_sum.11
  7.2 0.2 select_reduce_fusion.1
  7.4 0.1 reduce_sum.55
  7.5 0.1 copy.75
  7.6 0.1 copy.73
  7.7 0.1 mul.194
  7.8 0.8 copy.76
  8.6 0.1 reshape.96
  8.6 0.1 select_reduce_fusion
  8.7 0.7 convert_reduce_fusion
  9.4 0.0 collective-permute-done
  9.4 0.2 maximum_convert_fusion
  9.6 1.4 multiply_convert_fusion.1
  11.0 0.4 copy.68
  11.4 0.1 reshape.85
  11.5 1.5 convolution_convert_fusion.2
  13.1 16.5 %shard_map.163 = bf16[8,32,384]{2,1,0:T(8,128)(2,1)S(1)} custom-call(bf16[8,32,384]{2,1,0:T(8,128)(2,1)S(1)} %bitcast.76), custom_call_target="tpu_custom_call" | custom-call | tf_op jit(solution)/shard_map/pallas_call | solution.py:61
  29.6 0.1 reshape_reshape.4
  29.7 0.1 fusion.37
  29.8 0.9 fusion.36
  30.7 0.6 broadcast_in_dim.6.feed
  31.3 4.2 %shard_map.164 = f32[4,16,1024]{2,1,0:T(8,128)S(1)} custom-call(f32[4,64,1024]{2,1,0:T(8,128)S(1)} %get-tuple-element.16.step, f32[4,64,1024]{2,1,0:T(8,128)S(1)} %get-tuple-element.6.given, f32[4,64,16,128]{3,2,1,0:T(8,128)S(1)} %broadcast_in_dim.6.feed, f32[16,1024]{1,0:T(8,128)S(1)} %exponential_negate_fusion.decay), custom_call_target="tpu_custom_call" | custom-call | tf_op jit(solution)/shard_map/pallas_call | solution.py:400
  35.6 0.0 copy-start.3
  35.6 0.0 copy-start.14
  35.7 0.0 copy-start.15
  35.7 7.1 %all-gather.1 = bf16[16,16,1024]{2,1,0:T(8,128)(2,1)S(1)} all-gather(bf16[4,16,1024]{2,1,0:T(8,128)(2,1)S(1)} %convert_element_type.92), channel_id=3, replica_groups=mesh['seq'=4,'exp'=8] {'seq'}, dimensions={0}, use_global_device_ids=true | all-gather | bytes 655360 | tf_op jit(solution)/shard_map/all_gather | solution.py:466
  42.8 5.4 %all-gather.2 = f32[4,4,1024]{2,1,0:T(4,128)S(1)} all-gather(f32[1,4,1024]{2,1,0:T(4,128)S(1)} %bitcast.88), channel_id=2, replica_groups=mesh['seq'=4,'exp'=8] {'seq'}, dimensions={0}, use_global_device_ids=true | all-gather | bytes 81920 | tf_op jit(solution)/shard_map/all_gather | solution.py:465
  48.2 0.2 fusion.27.rest_0_
  48.4 0.6 broadcast_in_dim.8.rest_1_
  49.0 7.7 %shard_map.165 = f32[4,64,1024]{2,1,0:T(8,128)S(1)} custom-call(f32[4,64,1024]{2,1,0:T(8,128)S(1)} %get-tuple-element.16.step, f32[4,64,1024]{2,1,0:T(8,128)S(1)} %get-tuple-element.6.given, f32[4,64,16,128]{3,2,1,0:T(8,128)S(1)} %broadcast_in_dim.6.feed, f32[16,1024]{1,0:T(8,128)S(1)} %exponential_negate_fusion.decay, f32[4,16,1024]{2,1,0:T(8,128)S(1)} %fusion.27.rest_0_, ...), custom_call_target="tpu_custom_call" | custom-call | tf_op jit(solution)/shard_map/pallas_call | solution.py:400
  56.8 1.0 fusion.17
  57.8 0.4 copy.71
  58.2 0.1 reshape.87
  58.4 0.0 copy-start.2
  58.4 0.0 copy-start.13
  58.4 5.8 %convolution_convert_fusion = bf16[256,4096]{1,0:T(8,128)(2,1)S(1)} fusion(bf16[256,1024]{1,0:T(8,128)(2,1)S(1)} %reshape.87, bf16[1024,4096]{1,0:T(8,128)(2,1)} %param.26), kind=kOutput, calls=%fused_computation.8 | convolution fusion | flops 2148532224 | bytes 11010048 | tf_op jit(solution)/shard_map/dot_general | solution.py:479
  64.2 0.0 copy-start.4
  64.2 34.4 %shard_map.166 = f32[32,4096]{1,0:T(8,128)S(1)} custom-call(bf16[4,2,32,4096]{3,2,1,0:T(8,128)(2,1)S(1)} %bitcast.75), custom_call_target="tpu_custom_call" | custom-call | tf_op jit(solution)/shard_map/pallas_call | solution.py:61
  98.5 0.1 reshape.89
  98.7 0.6 multiply_reduce_fusion
  99.3 0.4 multiply_convert_fusion.2
  99.8 0.2 copy.77
  100.0 0.1 reshape.90
  100.1 0.5 convolution_convert_fusion.1
  100.5 32.9 %shard_map.167 = bf16[4,8,16,4096]{3,2,1,0:T(8,128)(2,1)S(1)} custom-call(bf16[8,16,4096]{2,1,0:T(8,128)(2,1)S(1)} %bitcast.74), custom_call_target="tpu_custom_call" | custom-call | tf_op jit(solution)/shard_map/pallas_call | solution.py:61
  133.4 18.5 %fusion.4 = f32[512,3072]{1,0:T(8,128)} fusion(bf16[512,4096]{1,0:T(8,128)(2,1)S(1)} %bitcast.70, bf16[1,4096,3072]{2,1,0:T(8,128)(2,1)} %param.31), kind=kOutput, calls=%fused_computation.4 | convolution fusion | flops 12884901888 | bytes 35651584 | tf_op jit(solution)/shard_map/dot_general | solution.py:501
  151.9 20.3 %multiply_convert_fusion.clone.4 = bf16[512,3072]{1,0:T(8,128)(2,1)} fusion(f32[512,3072]{1,0:T(8,128)} %fusion.4, bf16[512,4096]{1,0:T(8,128)(2,1)S(1)} %bitcast.71, bf16[1,4096,3072]{2,1,0:T(8,128)(2,1)} %param.32), kind=kOutput, calls=%fused_computation.6.clone.clone.clone.1 | convolution fusion | flops 12894339072 | bytes 38797312 | tf_op jit(solution)/shard_map/dot_general | solution.py:502
  172.3 18.9 %fusion.6 = bf16[512,4096]{1,0:T(8,128)(2,1)S(1)} fusion(bf16[1,3072,4096]{2,1,0:T(8,128)(2,1)} %param.33, bf16[512,3072]{1,0:T(8,128)(2,1)} %multiply_convert_fusion.clone.4), kind=kOutput, calls=%fused_computation.7 | convolution fusion | flops 12886999040 | bytes 32505856 | tf_op jit(solution)/shard_map/dot_general | solution.py:505
  191.1 38.2 %shard_map.168 = bf16[8,16,4096]{2,1,0:T(8,128)(2,1)S(1)} custom-call(bf16[4,8,16,4096]{3,2,1,0:T(8,128)(2,1)S(1)} %bitcast.72), custom_call_target="tpu_custom_call" | custom-call | tf_op jit(solution)/shard_map/pallas_call | solution.py:61
  229.3 0.8 fusion.11
  230.2 0.9 copy.79
  231.1 0.0 copy-done.1
  (30 shorter events, 0.1 us)
Async XLA Ops:
  0.0 29.8 %copy-start = (bf16[256,1024]{1,0:T(8,128)(2,1)S(1)}, bf16[256,1024]{1,0:T(8,128)(2,1)}, u32[]{:S(2)}) copy-start(bf16[256,1024]{1,0:T(8,128)(2,1)} %param.22) | copy-start | bytes 1572868
  1.3 28.5 %copy-start.16 = (f32[1024]{0:T(1024)S(1)}, f32[1024]{0:T(1024)}, u32[]{:S(2)}) copy-start(f32[1024]{0:T(1024)} %param.23) | copy-start | bytes 12292
  1.3 8.1 %collective-permute-start = (bf16[3,4,1024]{2,0,1:T(4,128)(2,1)S(1)}, bf16[3,4,1024]{2,0,1:T(4,128)(2,1)S(1)}, u32[]{:S(2)}, u32[]{:S(2)}) collective-permute-start(bf16[3,4,1024]{2,0,1:T(4,128)(2,1)S(1)} %slice.87), channel_id=1, source_target_pairs={{0,8},{8,16},{16,24},{1,9},{9,17},{17,25},{2,10},{10,18},{18,26},{... | collective-permute-start | bytes 73736 | tf_op jit(solution)/shard_map/ppermute | solution.py:21
  6.0 7.0 %copy-start.5 = (f32[1,1024]{1,0:T(1,128)}, f32[1,1024]{1,0:T(1,128)S(1)}, u32[]{:S(2)}) copy-start(f32[1,1024]{1,0:T(1,128)S(1)} %get-tuple-element.12) | copy-start | bytes 12292
  6.0 7.0 %copy-start.7 = (f32[1,1024]{1,0:T(1,128)}, f32[1,1024]{1,0:T(1,128)S(1)}, u32[]{:S(2)}) copy-start(f32[1,1024]{1,0:T(1,128)S(1)} %get-tuple-element.13) | copy-start | bytes 12292
  6.1 7.0 %copy-start.9 = (f32[1,1024]{1,0:T(1,128)}, f32[1,1024]{1,0:T(1,128)S(1)}, u32[]{:S(2)}) copy-start(f32[1,1024]{1,0:T(1,128)S(1)} %get-tuple-element.14) | copy-start | bytes 12292
  6.1 7.0 %copy-start.11 = (f32[1,1024]{1,0:T(1,128)}, f32[1,1024]{1,0:T(1,128)S(1)}, u32[]{:S(2)}) copy-start(f32[1,1024]{1,0:T(1,128)S(1)} %get-tuple-element.15) | copy-start | bytes 12292
  35.6 21.1 %copy-start.3 = (bf16[64,4,1024]{2,1,0:T(4,128)(2,1)S(1)}, bf16[64,4,1024]{2,1,0:T(4,128)(2,1)}, u32[]{:S(2)}) copy-start(bf16[64,4,1024]{2,1,0:T(4,128)(2,1)} %param.18) | copy-start | bytes 1572868
  35.6 21.1 %copy-start.6 = (f32[1,1024]{1,0:T(1,128)S(1)}, f32[1,1024]{1,0:T(1,128)}, u32[]{:S(2)}) copy-start(f32[1,1024]{1,0:T(1,128)} %copy-done.5) | copy-start | bytes 12292
  35.6 21.1 %copy-start.8 = (f32[1,1024]{1,0:T(1,128)S(1)}, f32[1,1024]{1,0:T(1,128)}, u32[]{:S(2)}) copy-start(f32[1,1024]{1,0:T(1,128)} %copy-done.7) | copy-start | bytes 12292
  35.6 21.1 %copy-start.10 = (f32[1,1024]{1,0:T(1,128)S(1)}, f32[1,1024]{1,0:T(1,128)}, u32[]{:S(2)}) copy-start(f32[1,1024]{1,0:T(1,128)} %copy-done.9) | copy-start | bytes 12292
  35.6 21.1 %copy-start.12 = (f32[1,1024]{1,0:T(1,128)S(1)}, f32[1,1024]{1,0:T(1,128)}, u32[]{:S(2)}) copy-start(f32[1,1024]{1,0:T(1,128)} %copy-done.11) | copy-start | bytes 12292
  35.6 21.1 %copy-start.14 = (f32[1024]{0:T(1024)S(1)}, f32[1024]{0:T(1024)}, u32[]{:S(2)}) copy-start(f32[1024]{0:T(1024)} %param.20) | copy-start | bytes 12292
  35.7 21.1 %copy-start.15 = (f32[1024]{0:T(1024)S(1)}, f32[1024]{0:T(1024)}, u32[]{:S(2)}) copy-start(f32[1024]{0:T(1024)} %param.25) | copy-start | bytes 12292
  58.4 40.3 %copy-start.2 = (bf16[8,4,4096]{2,1,0:T(4,128)(2,1)S(1)}, bf16[8,4,4096]{2,1,0:T(4,128)(2,1)}, u32[]{:S(2)}) copy-start(bf16[8,4,4096]{2,1,0:T(4,128)(2,1)} %param.27) | copy-start | bytes 786436
  58.4 41.0 %copy-start.13 = (f32[4096]{0:T(1024)S(1)}, f32[4096]{0:T(1024)}, u32[]{:S(2)}) copy-start(f32[4096]{0:T(1024)} %param.28) | copy-start | bytes 49156
  64.2 35.9 %copy-start.4 = (s32[128,32]{0,1:T(8,128)S(1)}, s32[128,32]{0,1:T(8,128)}, u32[]{:S(2)}) copy-start(s32[128,32]{0,1:T(8,128)} %convert_reduce_fusion) | copy-start | bytes 49156
  172.3 58.8 %copy-start.1 = (bf16[256,1024]{1,0:T(8,128)(2,1)S(1)}, bf16[256,1024]{1,0:T(8,128)(2,1)}, u32[]{:S(2)}) copy-start(bf16[256,1024]{1,0:T(8,128)(2,1)} %param.22) | copy-start | bytes 1572868
